TPU v7x, 512 devices: a whole 4x8x8 slice. The times are simulated.
512 devices in a mesh: ctx: 64 (over z, y_hi, core), head: 8 (over x, y_lo).
Axes of the slice: x: 4, y: 8 (y_hi: 4, y_lo: 2; y = y_hi * 2 + y_lo), z: 8, core: 2. Of those that a mesh axis runs over, the one named last changes fastest.
Arguments:
- query_rows: bfloat16 [32768, 4096], P('ctx', 'head'), may hold values from -43 to 43
- key_rows: bfloat16 [32768, 4096], P('ctx', 'head'), may hold values from -4 to 4
- value_rows: bfloat16 [32768, 4096], P('ctx', 'head'), may hold values from -16 to 16
- out_gain: float32 [4096], P('head'), may hold values from 0.5 to 1.5
Outputs:
- normed: bfloat16 [32768, 4096], P('ctx', 'head')
All inputs are finite; a program needn't handle non-finite values.
Results may differ from a plain program's by a relative error of at most 0.0085.
Values may be sent and summed in bfloat16 or wider, within the bound.
No kernel may reach another device: no remote copies, remote signals or barrier semaphores. Data moves between devices by JAX's collectives and lax.ppermute only.
A program may use at most 64 MiB of HBM per device.

v0:
```python
import math
import jax
import jax.numpy as jnp
from jax import lax
from jax.sharding import PartitionSpec as P

HEADS = 32
HEAD_DIM = 128
BLOCK = 256
SUMMARY = 16


def band_block(block_items):
    query_part, key_part, value_part = block_items
    scores = jnp.einsum(
        "qhd,khd->hqk", query_part, key_part, preferred_element_type=jnp.float32
    ) * HEAD_DIM ** (-0.5)
    causal = lax.broadcasted_iota(jnp.int32, (BLOCK, BLOCK), 0) >= lax.broadcasted_iota(
        jnp.int32, (BLOCK, BLOCK), 1
    )
    scores = jnp.where(causal[None], scores, -1e30)
    row_max = jnp.max(scores, axis=-1)
    weights = jnp.where(causal[None], jnp.exp(scores - row_max[..., None]), 0.0)
    row_sum = jnp.sum(weights, axis=-1)
    joint_acc = jnp.einsum(
        "hqk,khd->qhd", weights.astype(jnp.bfloat16), value_part, preferred_element_type=jnp.float32
    )
    return (row_max, row_sum, joint_acc)


def summary_update(run_state, query_set, set_blocks, key_sub, value_sub, first_row):
    sub_rows = key_sub.shape[0]
    key_block = (first_row + jnp.arange(sub_rows, dtype=jnp.int32)) // SUMMARY

    def update(group_state):
        old_max, old_sum, old_acc = group_state
        scores = jnp.einsum(
            "gqhd,khd->ghqk", query_set, key_sub, preferred_element_type=jnp.float32
        ) * HEAD_DIM ** (-0.5)
        allowed = (key_block[None, :] < set_blocks[:, None])[:, None, None, :]
        scores = jnp.where(allowed, scores, -1e30)
        joint_max = jnp.maximum(old_max, jnp.max(scores, axis=-1))
        weights = jnp.where(allowed, jnp.exp(scores - joint_max[..., None]), 0.0)
        shrink = jnp.exp(old_max - joint_max)
        new_sum = old_sum * shrink + jnp.sum(weights, axis=-1)
        new_acc = old_acc * jnp.transpose(shrink, (0, 2, 1))[..., None] + jnp.einsum(
            "ghqk,khd->gqhd",
            weights.astype(jnp.bfloat16),
            value_sub,
            preferred_element_type=jnp.float32,
        )
        return (joint_max, new_sum, new_acc)

    def unchanged(group_state):
        return group_state

    return lax.cond(first_row // SUMMARY < jnp.max(set_blocks), update, unchanged, run_state)


def sweep_rows(run_state, query_set, set_blocks, key_part, value_part):
    piece_rows, head_count = (key_part.shape[0], key_part.shape[1])
    sub_rows = math.gcd(piece_rows, 512)
    sub_count = piece_rows // sub_rows
    key_split = key_part.reshape(sub_count, sub_rows, head_count, HEAD_DIM)
    value_split = value_part.reshape(sub_count, sub_rows, head_count, HEAD_DIM)
    first_rows = jnp.arange(sub_count, dtype=jnp.int32) * sub_rows

    def inner(state, sub_items):
        key_sub, value_sub, first_row = sub_items
        return (summary_update(state, query_set, set_blocks, key_sub, value_sub, first_row), None)

    run_state, _ = lax.scan(inner, run_state, (key_split, value_split, first_rows))
    return run_state


def summary_pass(query_set, set_blocks, summary_keys, summary_values):
    group_count, _, head_count, _ = query_set.shape
    initial = (
        jnp.full((group_count, head_count, BLOCK), -1e30, jnp.float32),
        jnp.zeros((group_count, head_count, BLOCK), jnp.float32),
        jnp.zeros((group_count, BLOCK, head_count, HEAD_DIM), jnp.float32),
    )
    return sweep_rows(
        initial,
        query_set,
        set_blocks,
        lax.all_gather(summary_keys, "ctx", axis=0, tiled=True),
        lax.all_gather(summary_values, "ctx", axis=0, tiled=True),
    )


def local(query_rows, key_rows, value_rows, out_gain):
    row_count, width = query_rows.shape
    head_count = width // HEAD_DIM
    block_count = row_count // BLOCK
    my_index = lax.axis_index("ctx")
    block_shape = (block_count, BLOCK, head_count, HEAD_DIM)
    query_blocks = query_rows.reshape(block_shape)
    key_blocks = key_rows.reshape(block_shape)
    value_blocks = value_rows.reshape(block_shape)
    band_max, band_sum, band_acc = lax.map(band_block, (query_blocks, key_blocks, value_blocks))
    summary_keys = key_blocks[:, BLOCK - SUMMARY :].reshape(
        block_count * SUMMARY, head_count, HEAD_DIM
    )
    summary_values = value_blocks[:, BLOCK - SUMMARY :].reshape(
        block_count * SUMMARY, head_count, HEAD_DIM
    )
    local_blocks = my_index * block_count + jnp.arange(block_count, dtype=jnp.int32)
    summary_state = summary_pass(query_blocks, local_blocks, summary_keys, summary_values)
    far_max, far_sum, far_acc = summary_state
    joint_max = jnp.maximum(band_max, far_max)
    band_scale = jnp.exp(band_max - joint_max)
    far_scale = jnp.exp(far_max - joint_max)
    joint_sum = band_sum * band_scale + far_sum * far_scale
    joint_acc = (
        band_acc * jnp.transpose(band_scale, (0, 2, 1))[..., None]
        + far_acc * jnp.transpose(far_scale, (0, 2, 1))[..., None]
    )
    attended = joint_acc / jnp.transpose(joint_sum, (0, 2, 1))[..., None]
    attended = attended.reshape(row_count, width)
    squares = jnp.sum(attended * attended, axis=-1)
    row_totals = lax.psum(squares, "head")
    row_scale = lax.rsqrt(row_totals / (HEADS * HEAD_DIM) + 1e-06)
    return (attended * row_scale[:, None] * out_gain).astype(jnp.bfloat16)


def solution(mesh):
    placed = (P("ctx", "head"), P("ctx", "head"), P("ctx", "head"), P("head"))
    return jax.shard_map(
        local, mesh=mesh, in_specs=placed, out_specs=P("ctx", "head"), check_vma=False
    )
```

profile of v0, /device:TPU:464, one launch (start us, length us, event | category | flops | bytes accessed | tf_op | source)
XLA Modules:
  0.0 243.3 jit_solution(7592375874192132577)
XLA Ops:
  6.5 1.2 reshape.64
  7.7 0.6 copy.24
  8.4 2.0 reshape.65
  10.4 0.8 slice.9
  11.1 0.6 copy.25
  11.8 0.6 add_reduce_fusion
  12.4 1.2 reshape.63
  13.6 0.1 copy.27
  13.7 1.1 broadcast.81.clone3
  14.8 7.0 %while.32 = (s32[]{:T(128)}, f32[2,4,256]{2,0,1:T(2,128)S(1)}, f32[2,4,256]{2,0,1:T(2,128)S(1)}, f32[2,256,4,128]{3,1,0,2:T(8,128)}, bf16[2,256,4,128]{3,2,1,0:T...) while((s32[]{:T(128)}, f32[2,4,256]{2,0,1:T(2,128)S(1)}, ...), condition=%wide.region_3.4_spmd, body=%wide.region_0.3_spmd.sunk | while | flops 136640512 | bytes 8962169 | solution.py:101
  14.8 0.1 constant_dynamic-slice_fusion.6
  14.9 1.1 constant_dynamic-slice_fusion.5
  16.1 0.2 copy.69
  16.2 0.3 fusion.50
  16.6 0.2 fusion.51
  16.8 0.3 convolution_bitcast_fusion.2
  17.2 0.2 copy.70
  17.4 0.9 constant_dynamic-update-slice_fusion.2
  18.3 0.1 constant_dynamic-slice_fusion.6
  18.4 1.1 constant_dynamic-slice_fusion.5
  19.6 0.2 copy.69
  19.8 0.3 fusion.50
  20.1 0.2 fusion.51
  20.3 0.3 convolution_bitcast_fusion.2
  20.7 0.2 copy.70
  20.9 0.9 constant_dynamic-update-slice_fusion.2
  21.8 66.8 %all-gather.3.cloned.1.call-done = bf16[2048,4,128]{2,0,1:T(8,128)(2,1)} async-done(((bf16[32,4,128]{2,0,1:T(8,128)(2,1)}), bf16[2048,4,128]{2,0,1:T(8,128)(2,1)}) %all-gather.3.cloned.1.call-update) | async-done | bytes 2097168 | tf_op jit(solution)/shard_map/all_gather | solution.py:87
  88.6 1.7 copy.26
  90.3 78.9 %all-gather.5.cloned.1.call-done = bf16[2048,4,128]{2,0,1:T(8,128)(2,1)} async-done(((bf16[32,4,128]{2,0,1:T(8,128)(2,1)}), bf16[2048,4,128]{2,0,1:T(8,128)(2,1)}) %all-gather.5.cloned.1.call-update) | async-done | bytes 2097168 | tf_op jit(solution)/shard_map/all_gather | solution.py:88
  169.2 3.1 %copy.28 = bf16[4,512,4,128]{3,1,2,0:T(8,128)(2,1)} copy(bf16[4,512,4,128]{3,1,0,2:T(8,128)(2,1)} %bitcast.98) | data formatting | bytes 4194304
  172.3 1.1 broadcast.81.clone3.1
  173.4 40.3 %while.33 = (s32[]{:T(128)}, f32[2,4,256]{2,0,1:T(2,128)S(1)}, f32[2,4,256]{2,0,1:T(2,128)S(1)}, f32[2,256,4,128]{3,1,0,2:T(8,128)}, s32[4]{0:T(128)S(1)}, /*ind...) while((s32[]{:T(128)}, f32[2,4,256]{2,0,1:T(2,128)S(1)}, ...), condition=%wide.region_10.11_spmd.clone, body=%wide.region_5.10_spmd.clone.sunk | while | flops 551042048 | bytes 24787012 | solution.py:72
  173.4 0.6 dynamic_slice.60
  177.2 6.2 %conditional.3 = ((f32[2,4,256]{2,0,1:T(2,128)S(1)}, f32[2,4,256]{2,0,1:T(2,128)S(1)}, f32[2,256,4,128]{3,1,0,2:T(8,128)})) conditional(s32[]{:T(128)} %convert_element_type.34, (f32[2,4,256]{2,0,1:T(2,128)S(1)}, f32[2,4,256]{2,0,1:T(2,128)S(1)}, f32[2,256,4,128]{3,1,0,2:T(8,128)}) %tuple.82, (s32[]{:T(128)}, s32[512]{0:T(512)S(1)}, s32[]{:T(128)}, ...), branch_computations={%region_6.6_spmd, %region_7.9_spmd.clone} | conditional | flops 551042048 | bytes 24784512 | solution.py:57
  177.2 0.7 add_select_fusion
  178.0 0.1 broadcast_compare_fusion
  178.1 1.0 fusion.11
  179.1 3.2 %fusion.20 = f32[2,256,4,128]{3,1,0,2:T(8,128)S(1)} fusion(f32[4,512,2,256]{3,1,2,0:T(8,128)S(1)} %get-tuple-element.523, f32[2,4,256]{2,0,1:T(2,128)S(1)} %get-tuple-element.648, pred[2,512]{1,0:T(4,128)(4,1)S(1)} %broadcast_compare_fusion, f32[2,256,4,128]{3,1,0,2:T(8,128)S(1)} %copy-done, bf16[4,512,4,128]{3,1,2,0:T(8,128)(2,1)} %get-tuple-element.410, ...), kind=kOutput, calls=%fused_computation.27 | convolution fusion | flops 274202624 | bytes 6833664 | tf_op jit(solution)/shard_map/while/body/eval_jaxpr/cond/branch_1_fun/ghqk,khd->gqhd/dot_general | solution.py:46
  182.3 1.1 fusion.13
  183.5 0.6 dynamic_slice.60
  187.3 6.2 %conditional.3 = ((f32[2,4,256]{2,0,1:T(2,128)S(1)}, f32[2,4,256]{2,0,1:T(2,128)S(1)}, f32[2,256,4,128]{3,1,0,2:T(8,128)})) conditional(s32[]{:T(128)} %convert_element_type.34, (f32[2,4,256]{2,0,1:T(2,128)S(1)}, f32[2,4,256]{2,0,1:T(2,128)S(1)}, f32[2,256,4,128]{3,1,0,2:T(8,128)}) %tuple.82, (s32[]{:T(128)}, s32[512]{0:T(512)S(1)}, s32[]{:T(128)}, ...), branch_computations={%region_6.6_spmd, %region_7.9_spmd.clone} | conditional | flops 551042048 | bytes 24784512 | solution.py:57
  187.3 0.7 add_select_fusion
  188.1 0.1 broadcast_compare_fusion
  188.1 1.0 fusion.11
  189.2 3.2 %fusion.20 = f32[2,256,4,128]{3,1,0,2:T(8,128)S(1)} fusion(f32[4,512,2,256]{3,1,2,0:T(8,128)S(1)} %get-tuple-element.523, f32[2,4,256]{2,0,1:T(2,128)S(1)} %get-tuple-element.648, pred[2,512]{1,0:T(4,128)(4,1)S(1)} %broadcast_compare_fusion, f32[2,256,4,128]{3,1,0,2:T(8,128)S(1)} %copy-done, bf16[4,512,4,128]{3,1,2,0:T(8,128)(2,1)} %get-tuple-element.410, ...), kind=kOutput, calls=%fused_computation.27 | convolution fusion | flops 274202624 | bytes 6833664 | tf_op jit(solution)/shard_map/while/body/eval_jaxpr/cond/branch_1_fun/ghqk,khd->gqhd/dot_general | solution.py:46
  192.4 1.1 fusion.13
  193.6 0.6 dynamic_slice.60
  197.4 6.2 %conditional.3 = ((f32[2,4,256]{2,0,1:T(2,128)S(1)}, f32[2,4,256]{2,0,1:T(2,128)S(1)}, f32[2,256,4,128]{3,1,0,2:T(8,128)})) conditional(s32[]{:T(128)} %convert_element_type.34, (f32[2,4,256]{2,0,1:T(2,128)S(1)}, f32[2,4,256]{2,0,1:T(2,128)S(1)}, f32[2,256,4,128]{3,1,0,2:T(8,128)}) %tuple.82, (s32[]{:T(128)}, s32[512]{0:T(512)S(1)}, s32[]{:T(128)}, ...), branch_computations={%region_6.6_spmd, %region_7.9_spmd.clone} | conditional | flops 551042048 | bytes 24784512 | solution.py:57
  197.4 0.7 add_select_fusion
  198.1 0.1 broadcast_compare_fusion
  198.2 1.0 fusion.11
  199.2 3.2 %fusion.20 = f32[2,256,4,128]{3,1,0,2:T(8,128)S(1)} fusion(f32[4,512,2,256]{3,1,2,0:T(8,128)S(1)} %get-tuple-element.523, f32[2,4,256]{2,0,1:T(2,128)S(1)} %get-tuple-element.648, pred[2,512]{1,0:T(4,128)(4,1)S(1)} %broadcast_compare_fusion, f32[2,256,4,128]{3,1,0,2:T(8,128)S(1)} %copy-done, bf16[4,512,4,128]{3,1,2,0:T(8,128)(2,1)} %get-tuple-element.410, ...), kind=kOutput, calls=%fused_computation.27 | convolution fusion | flops 274202624 | bytes 6833664 | tf_op jit(solution)/shard_map/while/body/eval_jaxpr/cond/branch_1_fun/ghqk,khd->gqhd/dot_general | solution.py:46
  202.5 1.1 fusion.13
  203.6 0.6 dynamic_slice.60
  207.4 6.2 %conditional.3 = ((f32[2,4,256]{2,0,1:T(2,128)S(1)}, f32[2,4,256]{2,0,1:T(2,128)S(1)}, f32[2,256,4,128]{3,1,0,2:T(8,128)})) conditional(s32[]{:T(128)} %convert_element_type.34, (f32[2,4,256]{2,0,1:T(2,128)S(1)}, f32[2,4,256]{2,0,1:T(2,128)S(1)}, f32[2,256,4,128]{3,1,0,2:T(8,128)}) %tuple.82, (s32[]{:T(128)}, s32[512]{0:T(512)S(1)}, s32[]{:T(128)}, ...), branch_computations={%region_6.6_spmd, %region_7.9_spmd.clone} | conditional | flops 551042048 | bytes 24784512 | solution.py:57
  207.5 0.7 add_select_fusion
  208.2 0.1 broadcast_compare_fusion
  208.3 1.0 fusion.11
  209.3 3.2 %fusion.20 = f32[2,256,4,128]{3,1,0,2:T(8,128)S(1)} fusion(f32[4,512,2,256]{3,1,2,0:T(8,128)S(1)} %get-tuple-element.523, f32[2,4,256]{2,0,1:T(2,128)S(1)} %get-tuple-element.648, pred[2,512]{1,0:T(4,128)(4,1)S(1)} %broadcast_compare_fusion, f32[2,256,4,128]{3,1,0,2:T(8,128)S(1)} %copy-done, bf16[4,512,4,128]{3,1,2,0:T(8,128)(2,1)} %get-tuple-element.410, ...), kind=kOutput, calls=%fused_computation.27 | convolution fusion | flops 274202624 | bytes 6833664 | tf_op jit(solution)/shard_map/while/body/eval_jaxpr/cond/branch_1_fun/ghqk,khd->gqhd/dot_general | solution.py:46
  212.6 1.1 fusion.13
  213.7 2.4 multiply_reduce_fusion
  216.1 18.7 %psum.7 = f32[512]{0:T(512)S(1)} all-reduce(f32[512]{0:T(512)S(1)} %bitcast.107), channel_id=1, replica_groups=mesh['ctx'=64,'head'=8] {'head'}, use_global_device_ids=true, to_apply=%region_12.13 | all-reduce | flops 512 | bytes 4096 | tf_op jit(solution)/shard_map/psum | solution.py:122
  234.8 0.7 copy.33
  235.5 0.9 fusion.37
  (65 shorter events, 0.6 us)
Async XLA Ops:
  6.5 82.0 %all-gather.3.cloned.1.call-start = ((), (), s32[]{:S(2)}) async-start(), calls=%async_computation | async-start | bytes 2129920 | tf_op jit(solution)/shard_map/all_gather | solution.py:87
  8.4 160.9 %all-gather.5.cloned.1.call-start = ((), (), s32[]{:S(2)}) async-start(), calls=%async_computation.1 | async-start | bytes 2129920 | tf_op jit(solution)/shard_map/all_gather | solution.py:88
  177.2 1.8 copy-start
  182.3 1.1 copy-start.1
  187.3 1.8 copy-start
  192.4 1.1 copy-start.1
  197.4 1.8 copy-start
  202.5 1.1 copy-start.1
  207.5 1.8 copy-start
  212.5 1.1 copy-start.1
  213.7 21.8 %copy-start.2 = (f32[512]{0:T(512)S(1)}, f32[512]{0:T(512)}, u32[]{:S(2)}) copy-start(f32[512]{0:T(512)} %param.13) | copy-start | bytes 6148
Sparse Core Ops, SparseCore 0:
  10.6 77.9 all-gather.2
  91.8 77.3 all-gather.4
where the time goes:
time: 244 us; the launch traced here: 243 us
  waiting for transfers between devices  146 us (60%)
  local copies, waits for them, and re-layouts  21.7 us (9%)
  blocking collectives  18.7 us (8%)
  matrix products  18.1 us (7%)
  between operations  13.5 us (6%)
  loops' own time  13.4 us (5%)
  other arithmetic  12.1 us (5%)
    all_gather x1, waiting for transfers between devices, summary_pass(): lax.all_gather(summary_values, 'ctx', axis=0, tiled=True)  78.9 us
    all_gather x1, waiting for transfers between devices, summary_pass(): lax.all_gather(summary_keys, 'ctx', axis=0, tiled=True)  66.8 us
    psum x1, blocking collectives, local(): row_totals = lax.psum(squares, 'head')  18.7 us
    dot_general x4, matrix products, update(): jnp.einsum('ghqk,khd->gqhd', weights.astype(jnp.bfloat16), value_sub, pre...  12.9 us
    another operation x1, loops' own time, sweep_rows(): lax.scan(inner, run_state, (key_split, value_split, first_rows))  12.8 us
    unnamed x6, local copies, waits for them, and re-layouts  4.9 us
  transfers between devices with their start and end apart: 2, of which 2 were waited for; matrix products, arithmetic and copies ran while one was open for 6% of the time, Pallas kernels for 0%

commit v1 on v0

--- a/solution.py
+++ b/solution.py
@@ -119,7 +119,7 @@
     attended = joint_acc / jnp.transpose(joint_sum, (0, 2, 1))[..., None]
     attended = attended.reshape(row_count, width)
     squares = jnp.sum(attended * attended, axis=-1)
-    row_totals = lax.psum(squares, "head")
+    row_totals = jnp.sum(lax.all_gather(squares, "head"), axis=0)
     row_scale = lax.rsqrt(row_totals / (HEADS * HEAD_DIM) + 1e-06)
     return (attended * row_scale[:, None] * out_gain).astype(jnp.bfloat16)
 

time: 244 us -> 253 us (1.037)
  the two profiles are of different devices: /device:TPU:464 before, /device:TPU:400 now
where the time goes in v1:
time: 253 us
  waiting for transfers between devices  144 us (57%)
  local copies, waits for them, and re-layouts  27.3 us (11%)
  blocking collectives  24.6 us (10%)
  matrix products  17.8 us (7%)
  between operations  13.5 us (5%)
  loops' own time  13.3 us (5%)
  other arithmetic  11.8 us (5%)
    all_gather x1, waiting for transfers between devices, summary_pass(): lax.all_gather(summary_values, 'ctx', axis=0, tiled=True)  78.9 us
    all_gather x1, waiting for transfers between devices, summary_pass(): lax.all_gather(summary_keys, 'ctx', axis=0, tiled=True)  65.2 us
    all_gather x1, blocking collectives, local(): row_totals = jnp.sum(lax.all_gather(squares, 'head'), axis=0)  24.6 us
    another operation x1, loops' own time, sweep_rows(): lax.scan(inner, run_state, (key_split, value_split, first_rows))  12.8 us
    dot_general x4, matrix products, update(): jnp.einsum('ghqk,khd->gqhd', weights.astype(jnp.bfloat16), value_sub, pre...  12.5 us
  transfers between devices with their start and end apart: 2, of which 2 were waited for; matrix products, arithmetic and copies ran while one was open for 6% of the time, Pallas kernels for 0%

profile of v1, /device:TPU:400, one launch (start us, length us, event | category | flops | bytes accessed | tf_op | source)
XLA Modules:
  0.0 252.5 jit_solution(15911300963583469404)
XLA Ops:
  6.5 2.0 reshape.69
  8.5 0.8 slice.8
  9.3 0.6 copy.42
  9.9 2.0 reshape.70
  11.9 0.8 slice.9
  12.7 0.6 copy.43
  13.3 1.2 reshape.68
  14.5 0.7 add_reduce_fusion
  15.3 1.1 broadcast.88.clone3
  16.3 7.2 %while.32 = (s32[]{:T(128)}, f32[2,4,256]{2,0,1:T(2,128)S(1)}, f32[2,4,256]{2,0,1:T(2,128)S(1)}, f32[2,256,4,128]{3,1,0,2:T(8,128)}, bf16[2,256,4,128]{3,2,1,0:T...) while((s32[]{:T(128)}, f32[2,4,256]{2,0,1:T(2,128)S(1)}, ...), condition=%wide.region_3.4_spmd, body=%wide.region_0.3_spmd.sunk | while | flops 136640512 | bytes 8962169 | solution.py:101
  16.3 1.2 constant_dynamic-slice_fusion.5
  17.6 0.1 constant_dynamic-slice_fusion.6
  17.7 0.3 fusion.50
  18.1 0.2 fusion.51
  18.4 0.2 copy.87
  18.5 0.3 convolution_bitcast_fusion.2
  18.9 0.2 copy.88
  19.1 0.9 constant_dynamic-update-slice_fusion.2
  19.9 1.2 constant_dynamic-slice_fusion.5
  21.1 0.1 constant_dynamic-slice_fusion.6
  21.3 0.3 fusion.50
  21.7 0.2 fusion.51
  21.9 0.2 copy.87
  22.1 0.3 convolution_bitcast_fusion.2
  22.5 0.2 copy.88
  22.7 0.9 constant_dynamic-update-slice_fusion.2
  23.5 65.2 %all-gather.4.cloned.1.call-done = bf16[2048,4,128]{2,0,1:T(8,128)(2,1)} async-done(((bf16[32,4,128]{2,0,1:T(8,128)(2,1)}), bf16[2048,4,128]{2,0,1:T(8,128)(2,1)}) %all-gather.4.cloned.1.call-update) | async-done | bytes 2097168 | tf_op jit(solution)/shard_map/all_gather | solution.py:87
  88.8 1.7 copy.44
  90.5 78.9 %all-gather.6.cloned.1.call-done = bf16[2048,4,128]{2,0,1:T(8,128)(2,1)} async-done(((bf16[32,4,128]{2,0,1:T(8,128)(2,1)}), bf16[2048,4,128]{2,0,1:T(8,128)(2,1)}) %all-gather.6.cloned.1.call-update) | async-done | bytes 2097168 | tf_op jit(solution)/shard_map/all_gather | solution.py:88
  169.4 3.1 %copy.46 = bf16[4,512,4,128]{3,1,2,0:T(8,128)(2,1)} copy(bf16[4,512,4,128]{3,1,0,2:T(8,128)(2,1)} %bitcast.96) | data formatting | bytes 4194304
  172.6 1.1 broadcast.88.clone3.1
  173.6 43.3 %while.33 = (s32[]{:T(128)}, f32[2,4,256]{2,0,1:T(2,128)S(1)}, f32[2,4,256]{2,0,1:T(2,128)S(1)}, f32[2,256,4,128]{3,1,0,2:T(8,128)}, s32[4]{0:T(128)S(1)}, /*ind...) while((s32[]{:T(128)}, f32[2,4,256]{2,0,1:T(2,128)S(1)}, ...), condition=%wide.region_10.11_spmd.clone, body=%wide.region_5.10_spmd.clone.sunk | while | flops 551042048 | bytes 24787012 | solution.py:72
  173.6 0.6 dynamic_slice.60
  177.5 7.0 %conditional.3 = ((f32[2,4,256]{2,0,1:T(2,128)S(1)}, f32[2,4,256]{2,0,1:T(2,128)S(1)}, f32[2,256,4,128]{3,1,0,2:T(8,128)})) conditional(s32[]{:T(128)} %convert_element_type.34, (f32[2,4,256]{2,0,1:T(2,128)S(1)}, f32[2,4,256]{2,0,1:T(2,128)S(1)}, f32[2,256,4,128]{3,1,0,2:T(8,128)}) %tuple.84, (s32[]{:T(128)}, s32[512]{0:T(512)S(1)}, s32[]{:T(128)}, ...), branch_computations={%region_6.6_spmd, %region_7.9_spmd.clone} | conditional | flops 551042048 | bytes 24784512 | solution.py:57
  177.5 0.6 add_select_fusion
  178.2 1.0 fusion.11
  179.2 1.1 fusion.13
  180.3 3.1 %fusion.20 = f32[2,256,4,128]{3,1,0,2:T(8,128)S(1)} fusion(f32[4,512,2,256]{3,1,2,0:T(8,128)S(1)} %get-tuple-element.540, f32[2,4,256]{2,0,1:T(2,128)S(1)} %get-tuple-element.665, pred[2,512]{1,0:T(4,128)(4,1)S(1)} %broadcast_compare_fusion, f32[2,256,4,128]{3,1,0,2:T(8,128)S(1)} %copy-done, bf16[4,512,4,128]{3,1,2,0:T(8,128)(2,1)} %get-tuple-element.410, ...), kind=kOutput, calls=%fused_computation.27 | convolution fusion | flops 274202624 | bytes 6833664 | tf_op jit(solution)/shard_map/while/body/eval_jaxpr/cond/branch_1_fun/ghqk,khd->gqhd/dot_general | solution.py:46
  183.5 1.0 copy-done.1
  184.5 0.6 dynamic_slice.60
  188.3 7.0 %conditional.3 = ((f32[2,4,256]{2,0,1:T(2,128)S(1)}, f32[2,4,256]{2,0,1:T(2,128)S(1)}, f32[2,256,4,128]{3,1,0,2:T(8,128)})) conditional(s32[]{:T(128)} %convert_element_type.34, (f32[2,4,256]{2,0,1:T(2,128)S(1)}, f32[2,4,256]{2,0,1:T(2,128)S(1)}, f32[2,256,4,128]{3,1,0,2:T(8,128)}) %tuple.84, (s32[]{:T(128)}, s32[512]{0:T(512)S(1)}, s32[]{:T(128)}, ...), branch_computations={%region_6.6_spmd, %region_7.9_spmd.clone} | conditional | flops 551042048 | bytes 24784512 | solution.py:57
  188.3 0.6 add_select_fusion
  189.0 1.0 fusion.11
  190.1 1.1 fusion.13
  191.2 3.1 %fusion.20 = f32[2,256,4,128]{3,1,0,2:T(8,128)S(1)} fusion(f32[4,512,2,256]{3,1,2,0:T(8,128)S(1)} %get-tuple-element.540, f32[2,4,256]{2,0,1:T(2,128)S(1)} %get-tuple-element.665, pred[2,512]{1,0:T(4,128)(4,1)S(1)} %broadcast_compare_fusion, f32[2,256,4,128]{3,1,0,2:T(8,128)S(1)} %copy-done, bf16[4,512,4,128]{3,1,2,0:T(8,128)(2,1)} %get-tuple-element.410, ...), kind=kOutput, calls=%fused_computation.27 | convolution fusion | flops 274202624 | bytes 6833664 | tf_op jit(solution)/shard_map/while/body/eval_jaxpr/cond/branch_1_fun/ghqk,khd->gqhd/dot_general | solution.py:46
  194.3 1.0 copy-done.1
  195.3 0.6 dynamic_slice.60
  199.1 7.0 %conditional.3 = ((f32[2,4,256]{2,0,1:T(2,128)S(1)}, f32[2,4,256]{2,0,1:T(2,128)S(1)}, f32[2,256,4,128]{3,1,0,2:T(8,128)})) conditional(s32[]{:T(128)} %convert_element_type.34, (f32[2,4,256]{2,0,1:T(2,128)S(1)}, f32[2,4,256]{2,0,1:T(2,128)S(1)}, f32[2,256,4,128]{3,1,0,2:T(8,128)}) %tuple.84, (s32[]{:T(128)}, s32[512]{0:T(512)S(1)}, s32[]{:T(128)}, ...), branch_computations={%region_6.6_spmd, %region_7.9_spmd.clone} | conditional | flops 551042048 | bytes 24784512 | solution.py:57
  199.1 0.6 add_select_fusion
  199.9 1.0 fusion.11
  200.9 1.1 fusion.13
  202.0 3.1 %fusion.20 = f32[2,256,4,128]{3,1,0,2:T(8,128)S(1)} fusion(f32[4,512,2,256]{3,1,2,0:T(8,128)S(1)} %get-tuple-element.540, f32[2,4,256]{2,0,1:T(2,128)S(1)} %get-tuple-element.665, pred[2,512]{1,0:T(4,128)(4,1)S(1)} %broadcast_compare_fusion, f32[2,256,4,128]{3,1,0,2:T(8,128)S(1)} %copy-done, bf16[4,512,4,128]{3,1,2,0:T(8,128)(2,1)} %get-tuple-element.410, ...), kind=kOutput, calls=%fused_computation.27 | convolution fusion | flops 274202624 | bytes 6833664 | tf_op jit(solution)/shard_map/while/body/eval_jaxpr/cond/branch_1_fun/ghqk,khd->gqhd/dot_general | solution.py:46
  205.2 1.0 copy-done.1
  206.1 0.6 dynamic_slice.60
  210.0 7.0 %conditional.3 = ((f32[2,4,256]{2,0,1:T(2,128)S(1)}, f32[2,4,256]{2,0,1:T(2,128)S(1)}, f32[2,256,4,128]{3,1,0,2:T(8,128)})) conditional(s32[]{:T(128)} %convert_element_type.34, (f32[2,4,256]{2,0,1:T(2,128)S(1)}, f32[2,4,256]{2,0,1:T(2,128)S(1)}, f32[2,256,4,128]{3,1,0,2:T(8,128)}) %tuple.84, (s32[]{:T(128)}, s32[512]{0:T(512)S(1)}, s32[]{:T(128)}, ...), branch_computations={%region_6.6_spmd, %region_7.9_spmd.clone} | conditional | flops 551042048 | bytes 24784512 | solution.py:57
  210.0 0.6 add_select_fusion
  210.7 1.0 fusion.11
  211.7 1.1 fusion.13
  212.8 3.1 %fusion.20 = f32[2,256,4,128]{3,1,0,2:T(8,128)S(1)} fusion(f32[4,512,2,256]{3,1,2,0:T(8,128)S(1)} %get-tuple-element.540, f32[2,4,256]{2,0,1:T(2,128)S(1)} %get-tuple-element.665, pred[2,512]{1,0:T(4,128)(4,1)S(1)} %broadcast_compare_fusion, f32[2,256,4,128]{3,1,0,2:T(8,128)S(1)} %copy-done, bf16[4,512,4,128]{3,1,2,0:T(8,128)(2,1)} %get-tuple-element.410, ...), kind=kOutput, calls=%fused_computation.27 | convolution fusion | flops 274202624 | bytes 6833664 | tf_op jit(solution)/shard_map/while/body/eval_jaxpr/cond/branch_1_fun/ghqk,khd->gqhd/dot_general | solution.py:46
  216.0 1.0 copy-done.1
  217.0 2.4 multiply_reduce_fusion
  219.3 0.7 copy.51
  220.0 24.6 %all-gather = f32[8,1,512]{2,1,0:T(1,128)S(1)} all-gather(f32[1,1,512]{2,1,0:T(1,128)S(1)} %reshape.76), channel_id=1, replica_groups=mesh['ctx'=64,'head'=8] {'head'}, dimensions={0}, use_global_device_ids=true | all-gather | bytes 18432 | tf_op jit(solution)/shard_map/all_gather | solution.py:122
  244.7 0.9 fusion.37
  (66 shorter events, 1.0 us)
Async XLA Ops:
  6.5 82.2 %all-gather.4.cloned.1.call-start = ((), (), s32[]{:S(2)}) async-start(), calls=%async_computation | async-start | bytes 2129920 | tf_op jit(solution)/shard_map/all_gather | solution.py:87
  9.9 159.5 %all-gather.6.cloned.1.call-start = ((), (), s32[]{:S(2)}) async-start(), calls=%async_computation.1 | async-start | bytes 2129920 | tf_op jit(solution)/shard_map/all_gather | solution.py:88
  178.2 2.1 copy-start
  183.5 1.0 copy-start.1
  189.0 2.1 copy-start
  194.3 1.0 copy-start.1
  199.9 2.1 copy-start
  205.1 1.0 copy-start.1
  210.7 2.1 copy-start
  216.0 1.0 copy-start.1
  217.0 27.8 %copy-start.2 = (f32[512]{0:T(512)S(1)}, f32[512]{0:T(512)}, u32[]{:S(2)}) copy-start(f32[512]{0:T(512)} %param.13) | copy-start | bytes 6148
Sparse Core Ops, SparseCore 0:
  10.6 78.1 all-gather.3
  92.0 77.3 all-gather.5
